TPU v7x, 256 devices: a whole 4x4x8 slice. The times are simulated.
256 devices in a mesh: step: 32 (over y, z), ex: 8 (over x, core).
Axes of the slice: x: 4, y: 4, z: 8, core: 2. Of those that a mesh axis runs over, the one named last changes fastest.
Arguments:
- gradients: bfloat16 [256, 1024, 512], P('step', 'ex'), may hold values from -6 to 6, as said below
- step_rates: float32 [256], P('step'), may hold values from 0.02 to 0.08
Outputs:
- embeddings: float32 [256, 1024, 512], P('step', 'ex')
Inputs may be any that keep to these rules, and one draw needn't show every extreme that they name: real-valued projected gradients.
All inputs are finite; a program needn't handle non-finite values.
Results may differ from a plain program's by a relative error of at most 0.0003.
Values may be sent and summed in bfloat16 or wider, within the bound.
A program may use at most 128 MiB of HBM per device.

v0:
```python
import math

import jax
import jax.numpy as jnp
from jax import lax
from jax.sharding import PartitionSpec as P

P_SIZE = 512
BATCH = 1024


def carried_in(part, axis, combine, identity):
    count = lax.axis_size(axis)
    place = lax.axis_index(axis)
    ahead = count - 1 - place
    gathered = lax.all_gather(part, axis)
    state = jnp.zeros_like(part) + jnp.asarray(identity, part.dtype)

    def one(hop, state):
        source = count - 1 - hop
        return combine(state, lax.dynamic_index_in_dim(gathered, source, 0, False))

    return lax.fori_loop(0, ahead, one, state)


def gram_fragment(example_rows):
    return jnp.einsum(
        "sbp,sbq->spq", example_rows, example_rows, preferred_element_type=jnp.float32
    )


def per_device(gradients, step_rates):
    block_steps = gradients.shape[0]
    width = gradients.shape[2]
    spectral_edge = (math.sqrt(BATCH) + math.sqrt(P_SIZE)) ** 2
    identity = jnp.eye(width, dtype=jnp.float32)
    inner_products = lax.psum(gram_fragment(gradients), "ex")
    step_maps = identity[None, :, :] - (step_rates / spectral_edge)[:, None, None] * inner_products
    inside_region = [identity] * block_steps
    running = identity
    for index in range(block_steps - 1, -1, -1):
        inside_region[index] = running
        if index == block_steps - 1:
            running = step_maps[index]
        else:
            running = jnp.matmul(running, step_maps[index], precision=lax.Precision.HIGHEST)
    within_stack = jnp.stack(inside_region, axis=0)

    def chain_maps(earlier, trailing_segment):
        return jnp.matmul(earlier, trailing_segment, precision=lax.Precision.HIGHEST)

    outer_region = carried_in(running, "step", chain_maps, identity)
    broad_row_matrix = gradients.astype(jnp.float32)
    nested_segment = jnp.einsum(
        "sbp,sqp->sbq", broad_row_matrix, within_stack, precision=lax.Precision.HIGHEST
    )
    return jnp.einsum("kcn,tn->kct", nested_segment, outer_region, precision=lax.Precision.HIGHEST)


def solution(mesh):
    in_specs = (P("step", "ex", None), P("step"))
    out_specs = P("step", "ex", None)
    return jax.shard_map(
        per_device, mesh=mesh, in_specs=in_specs, out_specs=out_specs, check_vma=False
    )
```

profile of v0, /device:TPU:1, one launch (start us, length us, event | category | flops | bytes accessed | tf_op | source)
XLA Modules:
  0.0 494.2 jit_solution(17136038611669413283)
XLA Ops:
  6.5 1.2 copy-done
  7.8 4.5 fusion.16
  12.4 0.1 fusion.14
  12.5 0.3 copy.3
  12.8 0.1 copy-done.6
  12.9 112.0 %all-reduce.2.cloned.1.call-done = f32[8,512,512]{2,1,0:T(8,128)} async-done(((f32[8,512,512]{2,1,0:T(8,128)}), f32[8,512,512]{2,1,0:T(8,128)}) %all-reduce.2.cloned.1.call-update) | async-done | bytes 8388624 | tf_op jit(solution)/shard_map/psum | solution.py:37
  125.0 4.8 multiply_subtract_fusion
  129.8 1.8 fusion.11
  131.7 1.9 fusion.10
  133.5 1.0 copy-done.2
  134.5 1.9 fusion.9
  136.4 1.0 copy-done.3
  137.4 1.9 fusion.8
  139.2 1.0 copy-done.4
  140.3 1.9 fusion.7
  142.1 1.0 copy-done.5
  143.1 3.0 bitcast_dynamic-update-slice_fusion.5
  146.1 2.8 fusion.5
  149.0 2.3 bitcast_dynamic-update-slice_fusion.4
  151.4 2.2 bitcast_dynamic-update-slice_fusion.3
  153.6 2.3 bitcast_dynamic-update-slice_fusion.2
  155.9 2.3 bitcast_dynamic-update-slice_fusion.1
  158.2 1.1 bitcast_dynamic-update-slice_fusion
  159.2 2.3 slice_dynamic-update-slice_fusion
  161.5 1.1 convert_dynamic-update-slice_fusion
  162.6 9.9 %fusion.17 = f32[8,512,128]{1,2,0:T(8,128)} fusion(f32[8,512,512]{2,1,0:T(8,128)} %convert_dynamic-update-slice_fusion, bf16[8,128,512]{2,1,0:T(8,128)(2,1)S(1)} %copy-done), kind=kOutput, calls=%fused_computation.37 | convolution fusion | flops 3221225472 | bytes 11534336 | tf_op jit(solution)/shard_map/sbp,sqp->sbq/dot_general | solution.py:54
  172.5 209.7 %all-gather.3.cloned.1.call-done = f32[16384,512]{1,0:T(8,128)} async-done(((f32[512,512]{1,0:T(8,128)}), f32[16384,512]{1,0:T(8,128)}) %all-gather.3.cloned.1.call-update) | async-done | bytes 33554448 | tf_op jit(solution)/shard_map/all_gather | solution.py:16
  382.3 98.8 %while.12 = (s32[]{:T(128)}, f32[512,512]{0,1:T(8,128)S(1)}, s32[]{:T(128)}, f32[32,512,512]{2,1,0:T(8,128)}, s32[]{:T(128)}, /*index=5*/s32[]{:T(128)}, s32[]{:T(128)}, s32[]{:T(128)}) while((s32[]{:T(128)}, f32[512,512]{0,1:T(8,128)S(1)}, s32[]{:T(128)}, f32[32,512,512]{2,1,0:T(8,128)}, s32[]{:T(128)}, /*index=5*/s32[]{:T(128)}, s32[]{:T(128)}, ...), condition=%wide.region_2.3_spmd, body=%wide.region_1.2_spmd.sunk | while | flops 1610612736 | bytes 5243023 | solution.py:23
  382.3 3.1 convolution_bitcast_fusion.2
  385.4 0.1 copy.24
  385.5 3.1 convolution_bitcast_fusion.2
  388.6 0.1 copy.24
  388.7 3.1 convolution_bitcast_fusion.2
  391.8 0.1 copy.24
  391.9 3.1 convolution_bitcast_fusion.2
  395.0 0.1 copy.24
  395.1 3.1 convolution_bitcast_fusion.2
  398.3 3.1 convolution_bitcast_fusion.2
  401.5 3.1 convolution_bitcast_fusion.2
  404.6 3.1 convolution_bitcast_fusion.2
  407.8 3.1 convolution_bitcast_fusion.2
  411.0 3.1 convolution_bitcast_fusion.2
  414.2 3.1 convolution_bitcast_fusion.2
  417.4 3.1 convolution_bitcast_fusion.2
  420.6 3.1 convolution_bitcast_fusion.2
  423.8 3.1 convolution_bitcast_fusion.2
  426.9 3.1 convolution_bitcast_fusion.2
  430.1 3.1 convolution_bitcast_fusion.2
  433.3 3.1 convolution_bitcast_fusion.2
  436.5 3.1 convolution_bitcast_fusion.2
  439.7 3.1 convolution_bitcast_fusion.2
  442.9 3.1 convolution_bitcast_fusion.2
  446.1 3.1 convolution_bitcast_fusion.2
  449.3 3.1 convolution_bitcast_fusion.2
  452.4 3.1 convolution_bitcast_fusion.2
  455.6 3.1 convolution_bitcast_fusion.2
  458.8 3.1 convolution_bitcast_fusion.2
  462.0 3.1 convolution_bitcast_fusion.2
  465.2 3.1 convolution_bitcast_fusion.2
  468.4 3.1 convolution_bitcast_fusion.2
  471.6 3.1 convolution_bitcast_fusion.2
  474.7 3.1 convolution_bitcast_fusion.2
  477.9 3.1 convolution_bitcast_fusion.2
  481.0 6.3 %fusion.3 = f32[8,128,512]{2,1,0:T(8,128)} fusion(f32[8,512,128]{1,2,0:T(8,128)} %fusion.17, f32[512,512]{0,1:T(8,128)S(1)} %get-tuple-element.61), kind=kOutput, calls=%fused_computation.5 | convolution fusion | flops 3221225472 | bytes 5242880 | tf_op jit(solution)/shard_map/kcn,tn->kct/dot_general | solution.py:57
  (40 shorter events, 2.0 us)
Async XLA Ops:
  6.5 1.2 copy-start
  6.5 118.4 %all-reduce.2.cloned.1.call-start = ((), (), s32[]{:S(2)}) async-start(), calls=%async_computation | async-start | bytes 16777216 | tf_op jit(solution)/shard_map/psum | solution.py:37
  12.3 0.7 copy-start.6
  12.3 369.9 %all-gather.3.cloned.1.call-start = ((), (), s32[]{:S(2)}) async-start(), calls=%async_computation.1 | async-start | bytes 34603008 | tf_op jit(solution)/shard_map/all_gather | solution.py:16
  129.8 16.3 %copy-start.1 = (f32[8,512,512]{2,1,0:T(8,128)}, f32[8,512,512]{2,1,0:T(8,128)S(1)}, u32[]{:S(2)}) copy-start(f32[8,512,512]{2,1,0:T(8,128)S(1)} %multiply_subtract_fusion) | copy-start | bytes 25165828
  133.5 1.0 copy-start.2
  136.4 1.0 copy-start.3
  139.2 1.0 copy-start.4
  142.1 1.0 copy-start.5
Sparse Core Ops, SparseCore 0:
  12.4 112.4 all-reduce.1
  149.1 233.0 all-gather.2
where the time goes:
time: 496 us; the launch traced here: 494 us
  waiting for transfers between devices  322 us (65%)
  matrix products  131 us (26%)
  local copies, waits for them, and re-layouts  20.3 us (4%)
  between operations  13.5 us (3%)
  other arithmetic  6.05 us (1%)
    all_gather x1, waiting for transfers between devices, carried_in(): gathered = lax.all_gather(part, axis)  210 us
    psum x1, waiting for transfers between devices, per_device(): inner_products = lax.psum(gram_fragment(gradients), 'ex')  112 us
    dot_general x31, matrix products, chain_maps(): jnp.matmul(earlier, trailing_segment, precision=lax.Precision.HIGHEST)  95.5 us
    unnamed x20, local copies, waits for them, and re-layouts  17.8 us
    dot_general x7, matrix products, per_device(): jnp.matmul(running, step_maps[index], precision=lax.Precision.HIGHEST)  15.1 us
    dot_general x1, matrix products, per_device(): jnp.einsum('sbp,sqp->sbq', broad_row_matrix, within_stack, precision=lax....  9.93 us
  transfers between devices with their start and end apart: 2, of which 2 were waited for; matrix products, arithmetic and copies ran while one was open for 5% of the time, Pallas kernels for 0%

commit v1 on v0

v1 whole, which is shorter than its diff:
```python
import functools
import math

import jax
import jax.numpy as jnp
from jax import lax
from jax.experimental import pallas as pl
from jax.experimental.pallas import tpu as pltpu
from jax.sharding import PartitionSpec as P

P_SIZE = 512
BATCH = 1024
NX, NY, NZ = 4, 4, 8
STEPS_HERE = 8
EX_HERE = 128
TILE = 128
ABOVE = [(a, b) for a in range(4) for b in range(a + 1, 4)]
PAIRS = [(0, 1), (2, 3)]
PACK = 16 + (len(ABOVE) + len(PAIRS)) * TILE
CUT = PACK // 4 // 16 * 16
PARTS = ((0, CUT), (CUT, CUT), (2 * CUT, CUT), (3 * CUT, PACK - 3 * CUT))
PIECE = 64
F32, BF16 = jnp.float32, jnp.bfloat16
MESH = pl.DeviceIdType.MESH


def dot_nn(a, b):
    return lax.dot_general(a, b, (((1,), (0,)), ((), ())), preferred_element_type=F32)


def dot_tn(a, b):
    return lax.dot_general(a, b, (((0,), (0,)), ((), ())), preferred_element_type=F32)


def two_parts(v):
    hi = v.astype(BF16)
    return hi, (v - hi.astype(F32)).astype(BF16)


def eye_mask(rows, columns, row0):
    r = lax.broadcasted_iota(jnp.int32, (rows, columns), 0) + row0
    return r == lax.broadcasted_iota(jnp.int32, (rows, columns), 1)


def times_rows(x, diag, off_ref):
    n = x.shape[0]
    y = dot_nn(jnp.concatenate(two_parts(x), axis=0), off_ref[...])
    return x * diag + (y[:n] + y[n:])


def rows_plus_diag(diag, off_ref, start, n):
    return off_ref[pl.ds(start, n), :].astype(F32) + jnp.where(eye_mask(n, P_SIZE, start), diag, 0.0)


def rows_less_diag(x, diag, start):
    return (x - jnp.where(eye_mask(x.shape[0], P_SIZE, start), diag, 0.0)).astype(BF16)


def apply_part(x_ref, diag, off_ref, at, count):
    x = x_ref[pl.ds(at, count)].reshape(count * EX_HERE, P_SIZE)
    x = x * diag + dot_nn(x.astype(BF16), off_ref[...])
    x_ref[pl.ds(at, count)] = x.reshape(count, EX_HERE, P_SIZE)


def loop(first, last, run):
    def one(i, _):
        run(i)
        return 0

    lax.fori_loop(first, last, one, 0)


def choose(k, table):
    value = table[0]
    for i in range(1, len(table)):
        value = jnp.where(k == i, table[i], value)
    return value


def body(g_hbm, rate_hbm, out_ref, g_ref, rate_ref, gather, stage_r, stage_l, pack, maps, diags, v,
         mine, blocks, block_diags, mine_t, lines, line_diags,
         in_sem, g_send, g_recv, st_recv, p_send, p_recv,
         b_send, b_recv, bd_send, bd_recv, t_send, t_recv, td_send, td_recv):
    step, ex = lax.axis_index("step"), lax.axis_index("ex")
    y, z = step // NZ, step % NZ
    x, c = ex // 2, ex % 2
    xr, xl, xo = (x + 1) % NX, (x + 3) % NX, (x + 2) % NX
    sib = (step, x * 2 + 1 - c)
    right, left = (step, xr * 2 + c), (step, xl * 2 + c)
    z_next, z_prev = (y * NZ + (z + 1) % NZ, ex), (y * NZ + (z + NZ - 1) % NZ, ex)
    y_next, y_prev = (((y + 1) % NY) * NZ + z, ex), (((y + NY - 1) % NY) * NZ + z, ex)

    barrier = pltpu.get_barrier_semaphore()
    peers = [sib, right, left, (step, xr * 2 + 1 - c), (step, xl * 2 + 1 - c), z_next, z_prev, y_next, y_prev]
    for peer in peers:
        pl.semaphore_signal(barrier, inc=1, device_id=peer, device_id_type=MESH)
    pl.semaphore_wait(barrier, len(peers))

    def remote(src, dst, send, recv, device):
        return pltpu.make_async_remote_copy(
            src_ref=src, dst_ref=dst, send_sem=send, recv_sem=recv, device_id=device, device_id_type=MESH
        )

    started = []

    def go(copy):
        copy.start()
        started.append(copy)

    half = EX_HERE // 2

    def send_set(core):
        n = 1 + core * 6
        step_o, step_r, step_l = xo * 2 + core, xr * 2 + core, xl * 2 + core
        go(remote(g_hbm.at[step_o, pl.ds(0, half), :], stage_r.at[core], g_send.at[n], st_recv.at[core, 0], right))
        go(remote(g_hbm.at[step_o, pl.ds(half, half), :], stage_l.at[core], g_send.at[n + 1], st_recv.at[core, 1],
                  left))
        go(remote(g_hbm.at[step_r], gather.at[ex], g_send.at[n + 2], g_recv.at[ex, 0], (step, step_r)))
        go(remote(g_hbm.at[step_l], gather.at[ex], g_send.at[n + 3], g_recv.at[ex, 0], (step, step_l)))

    def forward_set(core):
        n = 1 + core * 6
        remote(stage_r.at[core], stage_r.at[core], g_send.at[0], st_recv.at[core, 0], sib).wait_recv()
        go(remote(stage_r.at[core], gather.at[xl * 2 + c, pl.ds(0, half), :], g_send.at[n + 4],
                  g_recv.at[xl * 2 + c, 0], (step, xr * 2 + core)))
        remote(stage_l.at[core], stage_l.at[core], g_send.at[0], st_recv.at[core, 1], sib).wait_recv()
        go(remote(stage_l.at[core], gather.at[xr * 2 + c, pl.ds(half, half), :], g_send.at[n + 5],
                  g_recv.at[xr * 2 + c, 1], (step, xl * 2 + core)))

    go(remote(g_hbm.at[x * 2 + 1 - c], gather.at[ex], g_send.at[0], g_recv.at[ex, 0], sib))
    send_set(0)
    own_in = pltpu.make_async_copy(g_hbm.at[ex], gather.at[ex], in_sem.at[0])
    all_in = pltpu.make_async_copy(g_hbm, g_ref, in_sem.at[1])
    rate_in = pltpu.make_async_copy(rate_hbm, rate_ref, in_sem.at[2])
    own_in.start()
    all_in.start()
    rate_in.start()
    forward_set(0)
    send_set(1)
    own_in.wait()
    rate_in.wait()

    def gram_of(chip, first):
        rows = gather[pl.ds(chip * 2, 2)].reshape(2 * EX_HERE, P_SIZE)
        if first:
            v[...] = dot_tn(rows, rows)
        else:
            v[...] += dot_tn(rows, rows)

    def arrived(source):
        remote(gather.at[source], gather.at[source], g_send.at[0], g_recv.at[source, 0], sib).wait_recv()

    def arrived_half(source, which):
        part = gather.at[source, pl.ds(which * half, half), :]
        remote(part, part, g_send.at[0], g_recv.at[source, which], sib).wait_recv()

    def gram_near():
        arrived(x * 2 + 1 - c)
        gram_of(x, True)

    def gram_far():
        for at in (xr, xl):
            for core in range(2):
                arrived(at * 2 + core)
            gram_of(at, False)
        for core in range(2):
            for which in range(2):
                arrived_half(xo * 2 + core, which)
        gram_of(xo, False)

    edge = (math.sqrt(BATCH) + math.sqrt(P_SIZE)) ** 2
    scale = rate_ref[ex] / edge
    own = pack.at[ex]
    row_at = lax.broadcasted_iota(jnp.int32, (TILE, TILE), 0)
    column_at = lax.broadcasted_iota(jnp.int32, (TILE, TILE), 1)
    on, upper, lower = row_at == column_at, row_at < column_at, row_at > column_at

    def pack_map():
        def map_tile(a, b):
            return v[pl.ds(a * TILE, TILE), pl.ds(b * TILE, TILE)] * (-scale)

        diag_parts = []
        for a in range(4):
            d = 1.0 + jnp.sum(jnp.where(on, map_tile(a, a), 0.0), axis=0, keepdims=True)
            d_hi, d_rest = d.astype(BF16).astype(F32), d - d.astype(BF16).astype(F32)
            d_mid = d_rest.astype(BF16).astype(F32)
            diag_parts.append((d_hi, d_mid, d_rest - d_mid))
        for n, (a, b) in enumerate(ABOVE):
            own[pl.ds(16 + n * TILE, TILE), :] = map_tile(a, b).astype(BF16)
        for n, (a, b) in enumerate(PAIRS):
            both = jnp.where(upper, map_tile(a, a), jnp.where(lower, map_tile(b, b), 0.0))
            own[pl.ds(16 + (len(ABOVE) + n) * TILE, TILE), :] = both.astype(BF16)
        rows = [diag_parts[a][part] for part in range(3) for a in range(4)]
        own[pl.ds(0, 16), :] = jnp.concatenate(rows + [jnp.zeros((4, TILE), F32)], axis=0).astype(BF16)

    def packed(slot, which):
        at, size = (0, PACK) if which == 4 else PARTS[which]
        return pack.at[slot, pl.ds(at, size), :]

    p_count = [0]

    def send_pack(slot, which, device):
        n = p_count[0]
        p_count[0] += 1
        go(remote(packed(slot, which), packed(slot, which), p_send.at[n], p_recv.at[slot, which], device))

    def got_pack(slot, which):
        remote(packed(slot, which), packed(slot, which), p_send.at[0], p_recv.at[slot, which], sib).wait_recv()

    def unpack(slot):
        parts = pack[slot, pl.ds(0, 16), :].astype(F32)
        diag = parts[0:4] + (parts[4:8] + parts[8:12])
        for a in range(4):
            diags[slot, :, pl.ds(a * TILE, TILE)] = diag[a:a + 1]

        def put(a, b, tile):
            maps[slot, pl.ds(a * TILE, TILE), pl.ds(b * TILE, TILE)] = tile

        for n, (a, b) in enumerate(ABOVE):
            tile = pack[slot, pl.ds(16 + n * TILE, TILE), :]
            put(a, b, tile)
            put(b, a, tile.T)
        for n, (a, b) in enumerate(PAIRS):
            tile = pack[slot, pl.ds(16 + (len(ABOVE) + n) * TILE, TILE), :].astype(F32)
            turned = tile.T
            put(a, a, jnp.where(upper, tile, turned).astype(BF16))
            put(b, b, jnp.where(lower, tile, turned).astype(BF16))

    first = []
    for which, device in ((0, left), (2, right), (1, left), (3, right), (2, left), (0, right), (3, left), (1, right),
                          (4, sib)):
        n = len(first)
        first.append(remote(packed(ex, which), packed(ex, which), p_send.at[n], p_recv.at[ex, which], device))
    p_count[0] = len(first)

    def send_first():
        for copy in first:
            copy.start()

    @pl.when(c == 0)
    def _():
        gram_near()
        gram_far()
        pack_map()

    @pl.when(c == 1)
    def _():
        gram_near()

    forward_set(1)

    @pl.when(c == 0)
    def _():
        send_first()

    @pl.when(c == 1)
    def _():
        gram_far()
        pack_map()
        send_first()

    started.extend(first)
    all_in.wait()
    from_right, from_left, across = xr * 2 + c, xl * 2 + c, xo * 2 + c
    unpack(ex)
    for s in range(STEPS_HERE):
        out_ref[s] = g_ref[s].astype(F32)

    def take(chip):
        got_pack(chip * 2 + 1 - c, 4)
        unpack(chip * 2 + 1 - c)

    @pl.when(c == 1)
    def _():
        take(x)

    def both(slot, which, device, device_0):
        send_pack(slot, which, device)
        n = p_count[0]
        p_count[0] += 1
        copy = remote(packed(slot, which), packed(slot, which), p_send.at[n], p_recv.at[slot, which], device_0)
        extra.append(copy)

        @pl.when(c == 1)
        def _():
            copy.start()

    extra = []
    for which in range(2):
        got_pack(from_right, which)
        both(from_right, which, left, (step, xl * 2))
        got_pack(from_left, 2 + which)
        both(from_left, 2 + which, right, (step, xr * 2))
    for which in range(2):
        got_pack(from_right, 2 + which)
        got_pack(from_left, which)
    send_pack(from_right, 4, sib)
    send_pack(from_left, 4, sib)
    unpack(from_right)
    unpack(from_left)

    @pl.when(c == 1)
    def _():
        take(xr)
        take(xl)

    for which in range(4):
        got_pack(across, which)
    over = remote(packed(across, 4), packed(across, 4), p_send.at[p_count[0]], p_recv.at[across, 4], sib)

    @pl.when(c == 0)
    def _():
        over.start()

    unpack(across)

    @pl.when(c == 0)
    def _():
        take(x)
        take(xr)
        take(xl)
        for which in range(4):
            got_pack(xo * 2 + 1, which)

    @pl.when(c == 1)
    def _():
        got_pack(xo * 2, 4)

    unpack(xo * 2 + 1 - c)

    quarters = (x % 2) * 2
    start = pl.multiple_of((c * 4 + quarters) * PIECE, 2 * PIECE)
    few = rows_plus_diag(diags[0], maps.at[0], start, 2 * PIECE)
    for s in range(1, STEPS_HERE):
        few = times_rows(few, diags[s], maps.at[s])
    block_diag = diags[0]
    for s in range(1, STEPS_HERE):
        block_diag = block_diag * diags[s]
    block_diags[z] = block_diag
    mine[...] = rows_less_diag(few, block_diag, start)
    blocks[z, pl.ds(start, 2 * PIECE), :] = mine[...]

    def single(j):
        apply_part(out_ref, diags[j * 2 + 1], maps.at[j * 2 + 1], j * 2, 1)

    def unit(u):
        s = choose(u, (2, 3, 4, 4, 5, 5, 6, 6, 6, 7, 7, 7))
        pair = choose(u, (0, 0, 0, 1, 0, 1, 0, 1, 2, 0, 1, 2))
        apply_part(out_ref, diags[s], maps.at[s], pair * 2, 2)

    def later(u):
        slot = z + 1 + u // 4
        apply_part(out_ref, block_diags[slot], blocks.at[slot], (u % 4) * 2, 2)

    units = 4 * (NZ - 1 - z)

    def later_units(first, last):
        loop(jnp.minimum(first, units), jnp.minimum(last, units), later)

    early = z < NZ // 2
    inner_done = jnp.where(early, 12, 5)

    def ring(own, buf, dbuf, n, pos, ahead, behind, send, recv, d_send, d_recv, own_too, before):
        a_at = jnp.where(x == 3, 1, 0)
        to_left = jnp.where(x == 1, 0, 1)
        base = c * 4 + quarters
        p_a, p_b = base + a_at, base + 1 - a_at
        turns = n // 2

        def rows(slot, at, count):
            return buf.at[slot, pl.ds(pl.multiple_of(at * PIECE, PIECE), count * PIECE), :]

        def pass_on(slot, at, count, kind, land, device, src=None):
            there = rows(slot, at, count)
            go(remote(there if src is None else src, there, send.at[slot, kind], recv.at[slot, land], device))

        def got(slot, at, count, land):
            there = rows(slot, at, count)
            remote(there, there, send.at[slot, 0], recv.at[slot, land], sib).wait_recv()

        def pass_diag(slot, kind, device):
            go(remote(dbuf.at[slot], dbuf.at[slot], d_send.at[slot, kind], d_recv.at[slot], device))

        def got_diag(slot):
            remote(dbuf.at[slot], dbuf.at[slot], d_send.at[slot, 0], d_recv.at[slot], sib).wait_recv()

        def part(src, at):
            return None if src is None else src.at[pl.ds(pl.multiple_of(at * PIECE, PIECE), PIECE), :]

        def left_copy(slot, src=None):
            there = rows(slot, base + to_left, 1)
            mine_there = part(src, to_left)
            return remote(there if src is None else mine_there, there, send.at[slot, 5],
                          recv.at[slot, 2 + to_left], left)

        def over_a(slot, src=None):
            pass_on(slot, p_a, 1, 4, 2 + a_at, right, part(src, a_at))
            copy = left_copy(slot, src)

            @pl.when(x % 2 == 1)
            def _():
                copy.start()

            started.append(copy)

        def over_b(slot, src=None):
            copy = left_copy(slot, src)

            @pl.when(x % 2 == 0)
            def _():
                copy.start()

        def to_sibling(slot, src=None):
            pass_on(slot, base, 2, 6, 4, sib, src)

        other = c * 4 + 2 - quarters

        def over_x(slot):
            got(slot, other, 1, 2)
            got(slot, other + 1, 1, 3)
            pass_on(slot, other, 2, 7, 5, sib)

        def got_all(slot):
            got(slot, (1 - c) * 4 + quarters, 2, 4)
            got(slot, (1 - c) * 4 + 2 - quarters, 2, 5)

        own_a, own_b = part(own, a_at), part(own, 1 - a_at)
        pass_on(pos, p_a, 1, 0, 0, ahead, own_a)
        pass_on(pos, p_b, 1, 3, 1, behind, own_b)
        pass_on(pos, p_b, 1, 1, 1, ahead, own_b)
        pass_on(pos, p_a, 1, 2, 0, behind, own_a)
        pass_diag(pos, 0, ahead)
        pass_diag(pos, 1, behind)
        if own_too:
            over_a(pos, own)
            over_b(pos, own)
            to_sibling(pos, own)

        waiting = [pos] if own_too else []
        for s in range(turns):
            last = s == turns - 1
            up, down = (pos + n - 1 - s) % n, (pos + 1 + s) % n
            before[s](got_all)
            got(up, p_a, 1, 0)
            if not last:
                pass_on(up, p_a, 1, 0, 0, ahead)
            over_a(up)
            got(down, p_b, 1, 1)
            if not last:
                pass_on(down, p_b, 1, 3, 1, behind)
            over_b(down)
            if last:
                to_sibling(up)
            else:
                got(up, p_b, 1, 1)
                if s < turns - 2:
                    pass_on(up, p_b, 1, 1, 1, ahead)
                over_b(up)
                got(down, p_a, 1, 0)
                if s < turns - 2:
                    pass_on(down, p_a, 1, 2, 0, behind)
                over_a(down)
                to_sibling(up)
                to_sibling(down)
            got_diag(up)
            if not last:
                pass_diag(up, 0, ahead)
                got_diag(down)
                if s < turns - 2:
                    pass_diag(down, 1, behind)
            for slot in waiting:
                over_x(slot)
            waiting = [up] if last else [up, down]
        before[turns](got_all)
        for slot in waiting:
            over_x(slot)

        return got_all

    def first_fill(got_all):
        loop(0, STEPS_HERE // 2, single)
        loop(0, inner_done, unit)

    def block_fill(d):
        def run(got_all):
            got_all((z + d) % NZ)

            @pl.when(early)
            def _():
                loop(4 * d - 4, 4 * d, later)

        return run

    def last_fill(got_all):
        got_all((z + 3) % NZ)
        for d in (0, 5, 6, 7):
            got_all((z + d) % NZ)

        @pl.when(early)
        def _():
            loop(8, 12, later)

    got_all = ring(mine, blocks, block_diags, NZ, z, z_next, z_prev, b_send, b_recv, bd_send, bd_recv, True,
                   [first_fill, lambda _: None, block_fill(1), block_fill(2), last_fill])

    farthest = (z + NZ // 2) % NZ

    @pl.when(z >= NZ // 2)
    def _():
        got_all(farthest)

    few = rows_plus_diag(block_diags[0], blocks.at[0], start, 2 * PIECE)
    for s in range(1, NZ // 2):
        few = times_rows(few, block_diags[s], blocks.at[s])

    @pl.when(early)
    def _():
        got_all(farthest)

    for s in range(NZ // 2, NZ):
        few = times_rows(few, block_diags[s], blocks.at[s])
    line_diag = block_diags[0]
    for s in range(1, NZ):
        line_diag = line_diag * block_diags[s]
    line_diags[y] = line_diag
    mine_t[...] = rows_less_diag(few, line_diag, start)

    done = jnp.where(early, 12, 0)

    def line_fill(got_all):
        loop(inner_done, 12, unit)
        later_units(done, done + 8)

    got_all = ring(mine_t, lines, line_diags, NY, y, y_next, y_prev, t_send, t_recv, td_send, td_recv, False,
                   [line_fill, lambda _: later_units(done + 8, done + 12), lambda _: None])
    later_units(done + 12, done + 28)

    for d in range(1, NY):
        got_all((y + d) % NY)

        @pl.when(y + d < NY)
        def _():
            for at in (0, 4):
                apply_part(out_ref, line_diags[(y + d) % NY], lines.at[(y + d) % NY], at, 4)

    for copy in started:
        copy.wait_send()

    @pl.when(c == 1)
    def _():
        for copy in extra:
            copy.wait_send()

    @pl.when(c == 0)
    def _():
        over.wait_send()


def per_device(gradients, step_rates):
    square = (P_SIZE, P_SIZE)
    dma = pltpu.SemaphoreType.DMA
    return pl.pallas_call(
        body,
        out_shape=jax.ShapeDtypeStruct(gradients.shape, F32),
        in_specs=[pl.BlockSpec(memory_space=pl.ANY)] * 2,
        out_specs=pl.BlockSpec(memory_space=pltpu.VMEM),
        scratch_shapes=[
            pltpu.VMEM((STEPS_HERE, EX_HERE, P_SIZE), BF16),
            pltpu.SMEM((STEPS_HERE,), F32),
            pltpu.VMEM((8, EX_HERE, P_SIZE), BF16),
            pltpu.VMEM((2, EX_HERE // 2, P_SIZE), BF16),
            pltpu.VMEM((2, EX_HERE // 2, P_SIZE), BF16),
            pltpu.VMEM((STEPS_HERE, PACK, TILE), BF16),
            pltpu.VMEM((STEPS_HERE,) + square, BF16),
            pltpu.VMEM((STEPS_HERE, 1, P_SIZE), F32),
            pltpu.VMEM(square, F32),
            pltpu.VMEM((2 * PIECE, P_SIZE), BF16),
            pltpu.VMEM((NZ,) + square, BF16),
            pltpu.VMEM((NZ, 1, P_SIZE), F32),
            pltpu.VMEM((2 * PIECE, P_SIZE), BF16),
            pltpu.VMEM((NY,) + square, BF16),
            pltpu.VMEM((NY, 1, P_SIZE), F32),
            dma((3,)),
            dma((13,)), dma((8, 2)), dma((2, 2)), dma((20,)), dma((8, 5)),
            dma((NZ, 8)), dma((NZ, 6)), dma((NZ, 2)), dma((NZ,)),
            dma((NY, 8)), dma((NY, 6)), dma((NY, 2)), dma((NY,)),
        ],
        compiler_params=pltpu.CompilerParams(
            collective_id=0, has_side_effects=True, vmem_limit_bytes=48 * 1024 * 1024
        ),
    )(pltpu.with_memory_space_constraint(gradients, pltpu.HBM),
      pltpu.with_memory_space_constraint(step_rates, pltpu.HBM))


def solution(mesh):
    in_specs = (P("step", "ex", None), P("step"))
    out_specs = P("step", "ex", None)
    return jax.shard_map(
        per_device, mesh=mesh, in_specs=in_specs, out_specs=out_specs, check_vma=False
    )
```

time: 496 us -> 76.3 us (0.15)
  waiting for transfers between devices: 322 us -> 0 us
  matrix products: 131 us -> 0 us
  Pallas kernels: 0 us -> 74.9 us
  local copies, waits for them, and re-layouts: 20.3 us -> 1.32 us
  between operations: 13.5 us -> 0.01 us
  other arithmetic: 6.05 us -> 0 us
    all_gather x1 -> x0, waiting for transfers between devices: 210 us -> none  [carried_in(): gathered = lax.all_gather(part, axis)]
    dot_general x41 -> x0, matrix products: 131 us -> none  [the longest x31 95.5 us: chain_maps(): jnp.matmul(earlier, trailing_segment, precision=lax.Precision.HIGHEST)]
    psum x1 -> x0, waiting for transfers between devices: 112 us -> none  [per_device(): inner_products = lax.psum(gram_fragment(gradients), 'ex')]
    pallas_call x0 -> x1, Pallas kernels: none -> 74.9 us  [per_device(): pl.pallas_call(body, out_shape=jax.ShapeDtypeStruct(gradients.shape, F32)...]
    unnamed x20 -> x1, local copies, waits for them, and re-layouts: 17.8 us -> 1.32 us
  transfers between devices with their start and end apart: 2 -> 0, of which waited for: 2 -> 0; matrix products, arithmetic and copies ran while one was open for 5% -> 0% of each run, Pallas kernels for 0% -> 0%
where the time goes in v1:
time: 76.3 us; the launch traced here: 76.2 us
  Pallas kernels  74.9 us (98%)
  local copies, waits for them, and re-layouts  1.32 us (2%)
    pallas_call x1, Pallas kernels, per_device(): pl.pallas_call(body, out_shape=jax.ShapeDtypeStruct(gradients.shape, F32)...  74.9 us

profile of v1, /device:TPU:1, one launch (start us, length us, event | category | flops | bytes accessed | tf_op | source)
XLA Modules:
  0.0 76.2 jit_solution(13872540256880668568)
XLA Ops:
  0.0 74.9 %shard_map.28 = f32[8,128,512]{2,1,0:T(8,128)S(1)} custom-call(bf16[8,128,512]{2,1,0:T(8,128)(2,1)} %g_hbm.1, f32[8]{0:T(128)} %rate_hbm.1), custom_call_target="tpu_custom_call" | custom-call | tf_op jit(solution)/shard_map/pallas_call | solution.py:562
  74.9 1.3 %copy.4 = f32[8,128,512]{2,1,0:T(8,128)} copy(f32[8,128,512]{2,1,0:T(8,128)S(1)} %shard_map.28) | data formatting | bytes 4194304

commit v2 on v1

--- a/solution.py
+++ b/solution.py
@@ -17,8 +17,8 @@
 ABOVE = [(a, b) for a in range(4) for b in range(a + 1, 4)]
 PAIRS = [(0, 1), (2, 3)]
 PACK = 16 + (len(ABOVE) + len(PAIRS)) * TILE
-CUT = PACK // 4 // 16 * 16
-PARTS = ((0, CUT), (CUT, CUT), (2 * CUT, CUT), (3 * CUT, PACK - 3 * CUT))
+CUT = PACK // 2 // 16 * 16
+PARTS = ((0, CUT), (CUT, PACK - CUT))
 PIECE = 64
 F32, BF16 = jnp.float32, jnp.bfloat16
 MESH = pl.DeviceIdType.MESH
@@ -42,18 +42,21 @@
     return r == lax.broadcasted_iota(jnp.int32, (rows, columns), 1)
 
 
-def times_rows(x, diag, off_ref):
+def times_rows(x_ref, diag, off_ref):
+    x = x_ref[...]
     n = x.shape[0]
     y = dot_nn(jnp.concatenate(two_parts(x), axis=0), off_ref[...])
-    return x * diag + (y[:n] + y[n:])
-
-
-def rows_plus_diag(diag, off_ref, start, n):
-    return off_ref[pl.ds(start, n), :].astype(F32) + jnp.where(eye_mask(n, P_SIZE, start), diag, 0.0)
-
-
-def rows_less_diag(x, diag, start):
-    return (x - jnp.where(eye_mask(x.shape[0], P_SIZE, start), diag, 0.0)).astype(BF16)
+    x_ref[...] = x * diag + (y[:n] + y[n:])
+
+
+def rows_plus_diag(x_ref, diag, off_ref, start):
+    n = x_ref.shape[0]
+    x_ref[...] = off_ref[pl.ds(start, n), :].astype(F32) + jnp.where(eye_mask(n, P_SIZE, start), diag, 0.0)
+
+
+def rows_less_diag(x_ref, diag, off_ref, start):
+    x = x_ref[...]
+    off_ref[...] = (x - jnp.where(eye_mask(x.shape[0], P_SIZE, start), diag, 0.0)).astype(BF16)
 
 
 def apply_part(x_ref, diag, off_ref, at, count):
@@ -77,8 +80,8 @@
     return value
 
 
-def body(g_hbm, rate_hbm, out_ref, g_ref, rate_ref, gather, stage_r, stage_l, pack, maps, diags, v,
-         mine, blocks, block_diags, mine_t, lines, line_diags,
+def body(g_hbm, rate_hbm, out_ref, last_ref, last_diag, g_ref, rate_ref, gather, stage_r, stage_l, pack, maps, diags, v,
+         few, mine, blocks, block_diags, mine_t, lines, line_diags,
          in_sem, g_send, g_recv, st_recv, p_send, p_recv,
          b_send, b_recv, bd_send, bd_recv, t_send, t_recv, td_send, td_recv):
     step, ex = lax.axis_index("step"), lax.axis_index("ex")
@@ -194,7 +197,7 @@
         own[pl.ds(0, 16), :] = jnp.concatenate(rows + [jnp.zeros((4, TILE), F32)], axis=0).astype(BF16)
 
     def packed(slot, which):
-        at, size = (0, PACK) if which == 4 else PARTS[which]
+        at, size = (0, PACK) if which == 2 else PARTS[which]
         return pack.at[slot, pl.ds(at, size), :]
 
     p_count = [0]
@@ -227,8 +230,7 @@
             put(b, b, jnp.where(lower, tile, turned).astype(BF16))
 
     first = []
-    for which, device in ((0, left), (2, right), (1, left), (3, right), (2, left), (0, right), (3, left), (1, right),
-                          (4, sib)):
+    for which, device in ((0, left), (1, right), (1, left), (0, right), (2, sib)):
         n = len(first)
         first.append(remote(packed(ex, which), packed(ex, which), p_send.at[n], p_recv.at[ex, which], device))
     p_count[0] = len(first)
@@ -267,35 +269,21 @@
         out_ref[s] = g_ref[s].astype(F32)
 
     def take(chip):
-        got_pack(chip * 2 + 1 - c, 4)
+        got_pack(chip * 2 + 1 - c, 2)
         unpack(chip * 2 + 1 - c)
 
     @pl.when(c == 1)
     def _():
         take(x)
 
-    def both(slot, which, device, device_0):
-        send_pack(slot, which, device)
-        n = p_count[0]
-        p_count[0] += 1
-        copy = remote(packed(slot, which), packed(slot, which), p_send.at[n], p_recv.at[slot, which], device_0)
-        extra.append(copy)
-
-        @pl.when(c == 1)
-        def _():
-            copy.start()
-
-    extra = []
-    for which in range(2):
-        got_pack(from_right, which)
-        both(from_right, which, left, (step, xl * 2))
-        got_pack(from_left, 2 + which)
-        both(from_left, 2 + which, right, (step, xr * 2))
-    for which in range(2):
-        got_pack(from_right, 2 + which)
-        got_pack(from_left, which)
-    send_pack(from_right, 4, sib)
-    send_pack(from_left, 4, sib)
+    got_pack(from_right, 0)
+    send_pack(from_right, 0, left)
+    got_pack(from_left, 1)
+    send_pack(from_left, 1, right)
+    got_pack(from_right, 1)
+    send_pack(from_right, 2, sib)
+    got_pack(from_left, 0)
+    send_pack(from_left, 2, sib)
     unpack(from_right)
     unpack(from_left)
 
@@ -304,14 +292,9 @@
         take(xr)
         take(xl)
 
-    for which in range(4):
+    for which in range(2):
         got_pack(across, which)
-    over = remote(packed(across, 4), packed(across, 4), p_send.at[p_count[0]], p_recv.at[across, 4], sib)
-
-    @pl.when(c == 0)
-    def _():
-        over.start()
-
+    send_pack(across, 2, sib)
     unpack(across)
 
     @pl.when(c == 0)
@@ -319,25 +302,19 @@
         take(x)
         take(xr)
         take(xl)
-        for which in range(4):
-            got_pack(xo * 2 + 1, which)
-
-    @pl.when(c == 1)
-    def _():
-        got_pack(xo * 2, 4)
-
-    unpack(xo * 2 + 1 - c)
+
+    take(xo)
 
     quarters = (x % 2) * 2
     start = pl.multiple_of((c * 4 + quarters) * PIECE, 2 * PIECE)
-    few = rows_plus_diag(diags[0], maps.at[0], start, 2 * PIECE)
+    rows_plus_diag(few, diags[0], maps.at[0], start)
     for s in range(1, STEPS_HERE):
-        few = times_rows(few, diags[s], maps.at[s])
+        times_rows(few, diags[s], maps.at[s])
     block_diag = diags[0]
     for s in range(1, STEPS_HERE):
         block_diag = block_diag * diags[s]
     block_diags[z] = block_diag
-    mine[...] = rows_less_diag(few, block_diag, start)
+    rows_less_diag(few, block_diag, mine, start)
     blocks[z, pl.ds(start, 2 * PIECE), :] = mine[...]
 
     def single(j):
@@ -509,21 +486,21 @@
     def _():
         got_all(farthest)
 
-    few = rows_plus_diag(block_diags[0], blocks.at[0], start, 2 * PIECE)
+    rows_plus_diag(few, block_diags[0], blocks.at[0], start)
     for s in range(1, NZ // 2):
-        few = times_rows(few, block_diags[s], blocks.at[s])
+        times_rows(few, block_diags[s], blocks.at[s])
 
     @pl.when(early)
     def _():
         got_all(farthest)
 
     for s in range(NZ // 2, NZ):
-        few = times_rows(few, block_diags[s], blocks.at[s])
+        times_rows(few, block_diags[s], blocks.at[s])
     line_diag = block_diags[0]
     for s in range(1, NZ):
         line_diag = line_diag * block_diags[s]
     line_diags[y] = line_diag
-    mine_t[...] = rows_less_diag(few, line_diag, start)
+    rows_less_diag(few, line_diag, mine_t, start)
 
     done = jnp.where(early, 12, 0)
 
@@ -536,34 +513,49 @@
     later_units(done + 12, done + 28)
 
     for d in range(1, NY):
-        got_all((y + d) % NY)
-
-        @pl.when(y + d < NY)
+        slot = (y + d) % NY
+        got_all(slot)
+
+        @pl.when(y + d < NY - 1)
         def _():
             for at in (0, 4):
-                apply_part(out_ref, line_diags[(y + d) % NY], lines.at[(y + d) % NY], at, 4)
+                apply_part(out_ref, line_diags[slot], lines.at[slot], at, 4)
+
+    @pl.when(y < NY - 1)
+    def _():
+        last_ref[...] = lines[NY - 1]
+        last_diag[...] = line_diags[NY - 1]
+
+    @pl.when(y == NY - 1)
+    def _():
+        last_ref[...] = jnp.zeros_like(last_ref)
+        last_diag[...] = jnp.ones_like(last_diag)
 
     for copy in started:
         copy.wait_send()
 
-    @pl.when(c == 1)
-    def _():
-        for copy in extra:
-            copy.wait_send()
-
-    @pl.when(c == 0)
-    def _():
-        over.wait_send()
+
+def finish(x_ref, off_ref, diag_ref, out_hbm, held, sem):
+    copies = []
+    for i in range(STEPS_HERE // 2):
+        x = x_ref[pl.ds(i * 2, 2)].reshape(2 * EX_HERE, P_SIZE)
+        x = x * diag_ref[...] + dot_nn(x.astype(BF16), off_ref[...])
+        held[pl.ds(i * 2, 2)] = x.reshape(2, EX_HERE, P_SIZE)
+        copies.append(pltpu.make_async_copy(held.at[pl.ds(i * 2, 2)], out_hbm.at[pl.ds(i * 2, 2)], sem.at[i]))
+        copies[-1].start()
+    for copy in copies:
+        copy.wait()
 
 
 def per_device(gradients, step_rates):
     square = (P_SIZE, P_SIZE)
     dma = pltpu.SemaphoreType.DMA
-    return pl.pallas_call(
+    rows, last, diag = pl.pallas_call(
         body,
-        out_shape=jax.ShapeDtypeStruct(gradients.shape, F32),
+        out_shape=[jax.ShapeDtypeStruct(gradients.shape, F32), jax.ShapeDtypeStruct(square, BF16),
+                   jax.ShapeDtypeStruct((1, P_SIZE), F32)],
         in_specs=[pl.BlockSpec(memory_space=pl.ANY)] * 2,
-        out_specs=pl.BlockSpec(memory_space=pltpu.VMEM),
+        out_specs=[pl.BlockSpec(memory_space=pltpu.VMEM)] * 3,
         scratch_shapes=[
             pltpu.VMEM((STEPS_HERE, EX_HERE, P_SIZE), BF16),
             pltpu.SMEM((STEPS_HERE,), F32),
@@ -574,6 +566,7 @@
             pltpu.VMEM((STEPS_HERE,) + square, BF16),
             pltpu.VMEM((STEPS_HERE, 1, P_SIZE), F32),
             pltpu.VMEM(square, F32),
+            pltpu.VMEM((2 * PIECE, P_SIZE), F32),
             pltpu.VMEM((2 * PIECE, P_SIZE), BF16),
             pltpu.VMEM((NZ,) + square, BF16),
             pltpu.VMEM((NZ, 1, P_SIZE), F32),
@@ -581,7 +574,7 @@
             pltpu.VMEM((NY,) + square, BF16),
             pltpu.VMEM((NY, 1, P_SIZE), F32),
             dma((3,)),
-            dma((13,)), dma((8, 2)), dma((2, 2)), dma((20,)), dma((8, 5)),
+            dma((13,)), dma((8, 2)), dma((2, 2)), dma((16,)), dma((8, 5)),
             dma((NZ, 8)), dma((NZ, 6)), dma((NZ, 2)), dma((NZ,)),
             dma((NY, 8)), dma((NY, 6)), dma((NY, 2)), dma((NY,)),
         ],
@@ -590,6 +583,14 @@
         ),
     )(pltpu.with_memory_space_constraint(gradients, pltpu.HBM),
       pltpu.with_memory_space_constraint(step_rates, pltpu.HBM))
+    return pl.pallas_call(
+        finish,
+        out_shape=jax.ShapeDtypeStruct(gradients.shape, F32),
+        in_specs=[pl.BlockSpec(memory_space=pltpu.VMEM)] * 3,
+        out_specs=pl.BlockSpec(memory_space=pl.ANY),
+        scratch_shapes=[pltpu.VMEM((STEPS_HERE, EX_HERE, P_SIZE), F32), dma((STEPS_HERE // 2,))],
+        compiler_params=pltpu.CompilerParams(vmem_limit_bytes=16 * 1024 * 1024),
+    )(rows, last, diag)
 
 
 def solution(mesh):

time: 76.3 us -> 75.6 us (level)
  local copies, waits for them, and re-layouts: 1.32 us -> 0 us
    unnamed x1 -> x0, local copies, waits for them, and re-layouts: 1.32 us -> none
    pallas_call x1 -> x2, Pallas kernels: 74.9 us -> 75.5 us  [the longest x1 73.8 us: per_device(): pl.pallas_call(body, out_shape=[jax.ShapeDtypeStruct(gradients.shape, F32...]
where the time goes in v2:
time: 75.6 us; the launch traced here: 75.5 us
  Pallas kernels  75.5 us (100%)
    pallas_call x1, Pallas kernels, per_device(): pl.pallas_call(body, out_shape=[jax.ShapeDtypeStruct(gradients.shape, F32...  73.8 us
    pallas_call x1, Pallas kernels, per_device(): pl.pallas_call(finish, out_shape=jax.ShapeDtypeStruct(gradients.shape, F3...  1.65 us

profile of v2, /device:TPU:1, one launch (start us, length us, event | category | flops | bytes accessed | tf_op | source)
XLA Modules:
  0.0 75.5 jit_solution(13918997976629994536)
XLA Ops:
  0.0 73.8 %shard_map.28 = (f32[8,128,512]{2,1,0:T(8,128)S(1)}, bf16[512,512]{1,0:T(8,128)(2,1)S(1)}, f32[1,512]{1,0:T(1,128)S(1)}) custom-call(bf16[8,128,512]{2,1,0:T(8,128)(2,1)} %g_hbm.1, f32[8]{0:T(128)} %rate_hbm.1), custom_call_target="tpu_custom_call" | custom-call | tf_op jit(solution)/shard_map/pallas_call | solution.py:553
  73.8 1.6 %shard_map.29 = f32[8,128,512]{2,1,0:T(8,128)} custom-call(f32[8,128,512]{2,1,0:T(8,128)S(1)} %get-tuple-element.8.x_ref, bf16[512,512]{1,0:T(8,128)(2,1)S(1)} %get-tuple-element.9.off_ref, f32[1,512]{1,0:T(1,128)S(1)} %get-tuple-element.10.diag_ref), custom_call_target="tpu_custom_call" | custom-call | tf_op jit(solution)/shard_map/pallas_call | solution.py:586

commit v3 on v2

--- a/solution.py
+++ b/solution.py
@@ -17,8 +17,8 @@
 ABOVE = [(a, b) for a in range(4) for b in range(a + 1, 4)]
 PAIRS = [(0, 1), (2, 3)]
 PACK = 16 + (len(ABOVE) + len(PAIRS)) * TILE
-CUT = PACK // 2 // 16 * 16
-PARTS = ((0, CUT), (CUT, PACK - CUT))
+CUT = PACK // 4 // 16 * 16
+PARTS = ((0, CUT), (CUT, CUT), (2 * CUT, CUT), (3 * CUT, PACK - 3 * CUT))
 PIECE = 64
 F32, BF16 = jnp.float32, jnp.bfloat16
 MESH = pl.DeviceIdType.MESH
@@ -109,6 +109,11 @@
     def go(copy):
         copy.start()
         started.append(copy)
+
+    def all_sent(count):
+        for copy in started[:count]:
+            copy.wait_send()
+        del started[:count]
 
     half = EX_HERE // 2
 
@@ -197,7 +202,7 @@
         own[pl.ds(0, 16), :] = jnp.concatenate(rows + [jnp.zeros((4, TILE), F32)], axis=0).astype(BF16)
 
     def packed(slot, which):
-        at, size = (0, PACK) if which == 2 else PARTS[which]
+        at, size = (0, PACK) if which == 4 else PARTS[which]
         return pack.at[slot, pl.ds(at, size), :]
 
     p_count = [0]
@@ -230,7 +235,8 @@
             put(b, b, jnp.where(lower, tile, turned).astype(BF16))
 
     first = []
-    for which, device in ((0, left), (1, right), (1, left), (0, right), (2, sib)):
+    for which, device in ((0, left), (2, right), (1, left), (3, right), (2, left), (0, right), (3, left), (1, right),
+                          (4, sib)):
         n = len(first)
         first.append(remote(packed(ex, which), packed(ex, which), p_send.at[n], p_recv.at[ex, which], device))
     p_count[0] = len(first)
@@ -269,21 +275,23 @@
         out_ref[s] = g_ref[s].astype(F32)
 
     def take(chip):
-        got_pack(chip * 2 + 1 - c, 2)
+        got_pack(chip * 2 + 1 - c, 4)
         unpack(chip * 2 + 1 - c)
 
     @pl.when(c == 1)
     def _():
         take(x)
 
-    got_pack(from_right, 0)
-    send_pack(from_right, 0, left)
-    got_pack(from_left, 1)
-    send_pack(from_left, 1, right)
-    got_pack(from_right, 1)
-    send_pack(from_right, 2, sib)
-    got_pack(from_left, 0)
-    send_pack(from_left, 2, sib)
+    for which in range(2):
+        got_pack(from_right, which)
+        send_pack(from_right, which, left)
+        got_pack(from_left, 2 + which)
+        send_pack(from_left, 2 + which, right)
+    for which in range(2):
+        got_pack(from_right, 2 + which)
+        got_pack(from_left, which)
+    send_pack(from_right, 4, sib)
+    send_pack(from_left, 4, sib)
     unpack(from_right)
     unpack(from_left)
 
@@ -292,9 +300,9 @@
         take(xr)
         take(xl)
 
-    for which in range(2):
+    for which in range(4):
         got_pack(across, which)
-    send_pack(across, 2, sib)
+    send_pack(across, 4, sib)
     unpack(across)
 
     @pl.when(c == 0)
@@ -454,9 +462,12 @@
 
         return got_all
 
+    before_ring = len(started)
+
     def first_fill(got_all):
         loop(0, STEPS_HERE // 2, single)
         loop(0, inner_done, unit)
+        all_sent(before_ring)
 
     def block_fill(d):
         def run(got_all):
@@ -503,10 +514,12 @@
     rows_less_diag(few, line_diag, mine_t, start)
 
     done = jnp.where(early, 12, 0)
+    before_line = len(started)
 
     def line_fill(got_all):
         loop(inner_done, 12, unit)
         later_units(done, done + 8)
+        all_sent(before_line)
 
     got_all = ring(mine_t, lines, line_diags, NY, y, y_next, y_prev, t_send, t_recv, td_send, td_recv, False,
                    [line_fill, lambda _: later_units(done + 8, done + 12), lambda _: None])
@@ -531,8 +544,7 @@
         last_ref[...] = jnp.zeros_like(last_ref)
         last_diag[...] = jnp.ones_like(last_diag)
 
-    for copy in started:
-        copy.wait_send()
+    all_sent(len(started))
 
 
 def finish(x_ref, off_ref, diag_ref, out_hbm, held, sem):

time: 75.6 us -> 75.1 us (level)
  no operation moved by 1% of the time
where the time goes in v3:
time: 75.1 us
  Pallas kernels  75 us (100%)
    pallas_call x1, Pallas kernels, per_device(): pl.pallas_call(body, out_shape=[jax.ShapeDtypeStruct(gradients.shape, F32...  73.4 us
    pallas_call x1, Pallas kernels, per_device(): pl.pallas_call(finish, out_shape=jax.ShapeDtypeStruct(gradients.shape, F3...  1.65 us

profile of v3, /device:TPU:1, one launch (start us, length us, event | category | flops | bytes accessed | tf_op | source)
XLA Modules:
  0.0 75.1 jit_solution(3031181652099372619)
XLA Ops:
  0.0 73.4 %shard_map.28 = (f32[8,128,512]{2,1,0:T(8,128)S(1)}, bf16[512,512]{1,0:T(8,128)(2,1)S(1)}, f32[1,512]{1,0:T(1,128)S(1)}) custom-call(bf16[8,128,512]{2,1,0:T(8,128)(2,1)} %g_hbm.1, f32[8]{0:T(128)} %rate_hbm.1), custom_call_target="tpu_custom_call" | custom-call | tf_op jit(solution)/shard_map/pallas_call | solution.py:565
  73.4 1.6 %shard_map.29 = f32[8,128,512]{2,1,0:T(8,128)} custom-call(f32[8,128,512]{2,1,0:T(8,128)S(1)} %get-tuple-element.8.x_ref, bf16[512,512]{1,0:T(8,128)(2,1)S(1)} %get-tuple-element.9.off_ref, f32[1,512]{1,0:T(1,128)S(1)} %get-tuple-element.10.diag_ref), custom_call_target="tpu_custom_call" | custom-call | tf_op jit(solution)/shard_map/pallas_call | solution.py:598

commit v4 on v3

--- a/solution.py
+++ b/solution.py
@@ -17,8 +17,7 @@
 ABOVE = [(a, b) for a in range(4) for b in range(a + 1, 4)]
 PAIRS = [(0, 1), (2, 3)]
 PACK = 16 + (len(ABOVE) + len(PAIRS)) * TILE
-CUT = PACK // 4 // 16 * 16
-PARTS = ((0, CUT), (CUT, CUT), (2 * CUT, CUT), (3 * CUT, PACK - 3 * CUT))
+PARTS = ((0, 16 + 2 * TILE),) + tuple((16 + at * TILE, 2 * TILE) for at in (2, 4, 6))
 PIECE = 64
 F32, BF16 = jnp.float32, jnp.bfloat16
 MESH = pl.DeviceIdType.MESH
@@ -32,31 +31,21 @@
     return lax.dot_general(a, b, (((0,), (0,)), ((), ())), preferred_element_type=F32)
 
 
-def two_parts(v):
-    hi = v.astype(BF16)
-    return hi, (v - hi.astype(F32)).astype(BF16)
-
-
-def eye_mask(rows, columns, row0):
-    r = lax.broadcasted_iota(jnp.int32, (rows, columns), 0) + row0
-    return r == lax.broadcasted_iota(jnp.int32, (rows, columns), 1)
-
-
-def times_rows(x_ref, diag, off_ref):
+def times_rows(x_ref, column, diag, off_ref, start):
     x = x_ref[...]
-    n = x.shape[0]
-    y = dot_nn(jnp.concatenate(two_parts(x), axis=0), off_ref[...])
-    x_ref[...] = x * diag + (y[:n] + y[n:])
-
-
-def rows_plus_diag(x_ref, diag, off_ref, start):
-    n = x_ref.shape[0]
-    x_ref[...] = off_ref[pl.ds(start, n), :].astype(F32) + jnp.where(eye_mask(n, P_SIZE, start), diag, 0.0)
-
-
-def rows_less_diag(x_ref, diag, off_ref, start):
-    x = x_ref[...]
-    off_ref[...] = (x - jnp.where(eye_mask(x.shape[0], P_SIZE, start), diag, 0.0)).astype(BF16)
+    here = off_ref[pl.ds(start, x.shape[0]), :].astype(F32)
+    x_ref[...] = (x * diag + column * here) + dot_nn(x.astype(BF16), off_ref[...])
+
+
+def running_diags(diag_ref, count, held, start):
+    product = diag_ref[0]
+    held[pl.ds(0, 1), :] = product
+    for s in range(1, count):
+        product = product * diag_ref[s]
+        held[pl.ds(s, 1), :] = product
+    rows = held[:, pl.ds(start, TILE)]
+    columns = jnp.concatenate([rows, jnp.zeros((TILE - rows.shape[0], TILE), F32)], axis=0).T
+    return product, [columns[:, s:s + 1] for s in range(count)]
 
 
 def apply_part(x_ref, diag, off_ref, at, count):
@@ -81,7 +70,7 @@
 
 
 def body(g_hbm, rate_hbm, out_ref, last_ref, last_diag, g_ref, rate_ref, gather, stage_r, stage_l, pack, maps, diags, v,
-         few, mine, blocks, block_diags, mine_t, lines, line_diags,
+         few, held, mine, blocks, block_diags, mine_t, lines, line_diags,
          in_sem, g_send, g_recv, st_recv, p_send, p_recv,
          b_send, b_recv, bd_send, bd_recv, t_send, t_recv, td_send, td_recv):
     step, ex = lax.axis_index("step"), lax.axis_index("ex")
@@ -150,10 +139,14 @@
 
     def gram_of(chip, first):
         rows = gather[pl.ds(chip * 2, 2)].reshape(2 * EX_HERE, P_SIZE)
+        mid = P_SIZE // 2
+        upper, lower = dot_tn(rows[:, :mid], rows), dot_tn(rows[:, mid:], rows[:, mid:])
         if first:
-            v[...] = dot_tn(rows, rows)
+            v[:mid, :] = upper
+            v[mid:, mid:] = lower
         else:
-            v[...] += dot_tn(rows, rows)
+            v[:mid, :] += upper
+            v[mid:, mid:] += lower
 
     def arrived(source):
         remote(gather.at[source], gather.at[source], g_send.at[0], g_recv.at[source, 0], sib).wait_recv()
@@ -183,23 +176,26 @@
     column_at = lax.broadcasted_iota(jnp.int32, (TILE, TILE), 1)
     on, upper, lower = row_at == column_at, row_at < column_at, row_at > column_at
 
-    def pack_map():
-        def map_tile(a, b):
-            return v[pl.ds(a * TILE, TILE), pl.ds(b * TILE, TILE)] * (-scale)
-
-        diag_parts = []
-        for a in range(4):
-            d = 1.0 + jnp.sum(jnp.where(on, map_tile(a, a), 0.0), axis=0, keepdims=True)
-            d_hi, d_rest = d.astype(BF16).astype(F32), d - d.astype(BF16).astype(F32)
-            d_mid = d_rest.astype(BF16).astype(F32)
-            diag_parts.append((d_hi, d_mid, d_rest - d_mid))
-        for n, (a, b) in enumerate(ABOVE):
-            own[pl.ds(16 + n * TILE, TILE), :] = map_tile(a, b).astype(BF16)
-        for n, (a, b) in enumerate(PAIRS):
-            both = jnp.where(upper, map_tile(a, a), jnp.where(lower, map_tile(b, b), 0.0))
-            own[pl.ds(16 + (len(ABOVE) + n) * TILE, TILE), :] = both.astype(BF16)
-        rows = [diag_parts[a][part] for part in range(3) for a in range(4)]
-        own[pl.ds(0, 16), :] = jnp.concatenate(rows + [jnp.zeros((4, TILE), F32)], axis=0).astype(BF16)
+    def map_tile(a, b):
+        return v[pl.ds(a * TILE, TILE), pl.ds(b * TILE, TILE)] * (-scale)
+
+    def pack_part(which):
+        if which == 0:
+            diag_parts = []
+            for a in range(4):
+                d = 1.0 + jnp.sum(jnp.where(on, map_tile(a, a), 0.0), axis=0, keepdims=True)
+                d_hi, d_rest = d.astype(BF16).astype(F32), d - d.astype(BF16).astype(F32)
+                d_mid = d_rest.astype(BF16).astype(F32)
+                diag_parts.append((d_hi, d_mid, d_rest - d_mid))
+            rows = [diag_parts[a][part] for part in range(3) for a in range(4)]
+            own[pl.ds(0, 16), :] = jnp.concatenate(rows + [jnp.zeros((4, TILE), F32)], axis=0).astype(BF16)
+        for n in (2 * which, 2 * which + 1):
+            if n < len(ABOVE):
+                tile = map_tile(*ABOVE[n])
+            else:
+                a, b = PAIRS[n - len(ABOVE)]
+                tile = jnp.where(upper, map_tile(a, a), jnp.where(lower, map_tile(b, b), 0.0))
+            own[pl.ds(16 + n * TILE, TILE), :] = tile.astype(BF16)
 
     def packed(slot, which):
         at, size = (0, PACK) if which == 4 else PARTS[which]
@@ -215,24 +211,31 @@
     def got_pack(slot, which):
         remote(packed(slot, which), packed(slot, which), p_send.at[0], p_recv.at[slot, which], sib).wait_recv()
 
-    def unpack(slot):
-        parts = pack[slot, pl.ds(0, 16), :].astype(F32)
-        diag = parts[0:4] + (parts[4:8] + parts[8:12])
-        for a in range(4):
-            diags[slot, :, pl.ds(a * TILE, TILE)] = diag[a:a + 1]
-
+    def unpack_part(slot, which):
         def put(a, b, tile):
             maps[slot, pl.ds(a * TILE, TILE), pl.ds(b * TILE, TILE)] = tile
 
-        for n, (a, b) in enumerate(ABOVE):
+        if which == 0:
+            parts = pack[slot, pl.ds(0, 16), :].astype(F32)
+            diag = parts[0:4] + (parts[4:8] + parts[8:12])
+            for a in range(4):
+                diags[slot, :, pl.ds(a * TILE, TILE)] = diag[a:a + 1]
+        for n in (2 * which, 2 * which + 1):
             tile = pack[slot, pl.ds(16 + n * TILE, TILE), :]
-            put(a, b, tile)
-            put(b, a, tile.T)
-        for n, (a, b) in enumerate(PAIRS):
-            tile = pack[slot, pl.ds(16 + (len(ABOVE) + n) * TILE, TILE), :].astype(F32)
-            turned = tile.T
-            put(a, a, jnp.where(upper, tile, turned).astype(BF16))
-            put(b, b, jnp.where(lower, tile, turned).astype(BF16))
+            if n < len(ABOVE):
+                a, b = ABOVE[n]
+                put(a, b, tile)
+                put(b, a, tile.T)
+            else:
+                a, b = PAIRS[n - len(ABOVE)]
+                tile = tile.astype(F32)
+                turned = tile.T
+                put(a, a, jnp.where(upper, tile, turned).astype(BF16))
+                put(b, b, jnp.where(lower, tile, turned).astype(BF16))
+
+    def unpack(slot):
+        for which in range(4):
+            unpack_part(slot, which)
 
     first = []
     for which, device in ((0, left), (2, right), (1, left), (3, right), (2, left), (0, right), (3, left), (1, right),
@@ -241,6 +244,10 @@
         first.append(remote(packed(ex, which), packed(ex, which), p_send.at[n], p_recv.at[ex, which], device))
     p_count[0] = len(first)
 
+    def pack_all():
+        for which in range(4):
+            pack_part(which)
+
     def send_first():
         for copy in first:
             copy.start()
@@ -249,7 +256,7 @@
     def _():
         gram_near()
         gram_far()
-        pack_map()
+        pack_all()
 
     @pl.when(c == 1)
     def _():
@@ -264,8 +271,11 @@
     @pl.when(c == 1)
     def _():
         gram_far()
-        pack_map()
-        send_first()
+        for which, copy in zip((0, 2, 1, 3), first):
+            pack_part(which)
+            copy.start()
+        for copy in first[4:]:
+            copy.start()
 
     started.extend(first)
     all_in.wait()
@@ -302,7 +312,7 @@
 
     for which in range(4):
         got_pack(across, which)
-    send_pack(across, 4, sib)
+        send_pack(across, which, sib)
     unpack(across)
 
     @pl.when(c == 0)
@@ -311,18 +321,18 @@
         take(xr)
         take(xl)
 
-    take(xo)
+    for which in range(4):
+        got_pack(xo * 2 + 1 - c, which)
+        unpack_part(xo * 2 + 1 - c, which)
 
     quarters = (x % 2) * 2
     start = pl.multiple_of((c * 4 + quarters) * PIECE, 2 * PIECE)
-    rows_plus_diag(few, diags[0], maps.at[0], start)
+    block_diag, columns = running_diags(diags, STEPS_HERE, held, start)
+    few[...] = maps[0, pl.ds(start, 2 * PIECE), :].astype(F32)
     for s in range(1, STEPS_HERE):
-        times_rows(few, diags[s], maps.at[s])
-    block_diag = diags[0]
-    for s in range(1, STEPS_HERE):
-        block_diag = block_diag * diags[s]
+        times_rows(few, columns[s - 1], diags[s], maps.at[s], start)
     block_diags[z] = block_diag
-    rows_less_diag(few, block_diag, mine, start)
+    mine[...] = few[...].astype(BF16)
     blocks[z, pl.ds(start, 2 * PIECE), :] = mine[...]
 
     def single(j):
@@ -492,26 +502,24 @@
                    [first_fill, lambda _: None, block_fill(1), block_fill(2), last_fill])
 
     farthest = (z + NZ // 2) % NZ
+    line_diag, columns = running_diags(block_diags, NZ, held, start)
 
     @pl.when(z >= NZ // 2)
     def _():
         got_all(farthest)
 
-    rows_plus_diag(few, block_diags[0], blocks.at[0], start)
+    few[...] = blocks[0, pl.ds(start, 2 * PIECE), :].astype(F32)
     for s in range(1, NZ // 2):
-        times_rows(few, block_diags[s], blocks.at[s])
+        times_rows(few, columns[s - 1], block_diags[s], blocks.at[s], start)
 
     @pl.when(early)
     def _():
         got_all(farthest)
 
     for s in range(NZ // 2, NZ):
-        times_rows(few, block_diags[s], blocks.at[s])
-    line_diag = block_diags[0]
-    for s in range(1, NZ):
-        line_diag = line_diag * block_diags[s]
+        times_rows(few, columns[s - 1], block_diags[s], blocks.at[s], start)
     line_diags[y] = line_diag
-    rows_less_diag(few, line_diag, mine_t, start)
+    mine_t[...] = few[...].astype(BF16)
 
     done = jnp.where(early, 12, 0)
     before_line = len(started)
@@ -579,6 +587,7 @@
             pltpu.VMEM((STEPS_HERE, 1, P_SIZE), F32),
             pltpu.VMEM(square, F32),
             pltpu.VMEM((2 * PIECE, P_SIZE), F32),
+            pltpu.VMEM((8, P_SIZE), F32),
             pltpu.VMEM((2 * PIECE, P_SIZE), BF16),
             pltpu.VMEM((NZ,) + square, BF16),
             pltpu.VMEM((NZ, 1, P_SIZE), F32),
@@ -586,7 +595,7 @@
             pltpu.VMEM((NY,) + square, BF16),
             pltpu.VMEM((NY, 1, P_SIZE), F32),
             dma((3,)),
-            dma((13,)), dma((8, 2)), dma((2, 2)), dma((16,)), dma((8, 5)),
+            dma((13,)), dma((8, 2)), dma((2, 2)), dma((19,)), dma((8, 5)),
             dma((NZ, 8)), dma((NZ, 6)), dma((NZ, 2)), dma((NZ,)),
             dma((NY, 8)), dma((NY, 6)), dma((NY, 2)), dma((NY,)),
         ],

time: 75.1 us -> 74.1 us (0.987)
  Pallas kernels: 75 us -> 74 us
    pallas_call x1, Pallas kernels: 73.4 us -> 72.4 us  [per_device(): pl.pallas_call(body, out_shape=[jax.ShapeDtypeStruct(gradients.shape, F32...]
where the time goes in v4:
time: 74.1 us; the launch traced here: 74 us
  Pallas kernels  74 us (100%)
    pallas_call x1, Pallas kernels, per_device(): pl.pallas_call(body, out_shape=[jax.ShapeDtypeStruct(gradients.shape, F32...  72.4 us
    pallas_call x1, Pallas kernels, per_device(): pl.pallas_call(finish, out_shape=jax.ShapeDtypeStruct(gradients.shape, F3...  1.65 us

profile of v4, /device:TPU:1, one launch (start us, length us, event | category | flops | bytes accessed | tf_op | source)
XLA Modules:
  0.0 74.0 jit_solution(12048209549831740607)
XLA Ops:
  0.0 72.4 %shard_map.28 = (f32[8,128,512]{2,1,0:T(8,128)S(1)}, bf16[512,512]{1,0:T(8,128)(2,1)S(1)}, f32[1,512]{1,0:T(1,128)S(1)}) custom-call(bf16[8,128,512]{2,1,0:T(8,128)(2,1)} %g_hbm.1, f32[8]{0:T(128)} %rate_hbm.1), custom_call_target="tpu_custom_call" | custom-call | tf_op jit(solution)/shard_map/pallas_call | solution.py:573
  72.4 1.6 %shard_map.29 = f32[8,128,512]{2,1,0:T(8,128)} custom-call(f32[8,128,512]{2,1,0:T(8,128)S(1)} %get-tuple-element.8.x_ref, bf16[512,512]{1,0:T(8,128)(2,1)S(1)} %get-tuple-element.9.off_ref, f32[1,512]{1,0:T(1,128)S(1)} %get-tuple-element.10.diag_ref), custom_call_target="tpu_custom_call" | custom-call | tf_op jit(solution)/shard_map/pallas_call | solution.py:607

commit v5 on v4

--- a/solution.py
+++ b/solution.py
@@ -477,19 +477,17 @@
     def first_fill(got_all):
         loop(0, STEPS_HERE // 2, single)
         loop(0, inner_done, unit)
-        all_sent(before_ring)
-
-    def block_fill(d):
-        def run(got_all):
+
+    def block_fill(got_all):
+        for d in (1, 2):
             got_all((z + d) % NZ)
 
             @pl.when(early)
             def _():
                 loop(4 * d - 4, 4 * d, later)
 
-        return run
-
     def last_fill(got_all):
+        all_sent(before_ring)
         got_all((z + 3) % NZ)
         for d in (0, 5, 6, 7):
             got_all((z + d) % NZ)
@@ -499,7 +497,7 @@
             loop(8, 12, later)
 
     got_all = ring(mine, blocks, block_diags, NZ, z, z_next, z_prev, b_send, b_recv, bd_send, bd_recv, True,
-                   [first_fill, lambda _: None, block_fill(1), block_fill(2), last_fill])
+                   [first_fill, lambda _: None, lambda _: None, block_fill, last_fill])
 
     farthest = (z + NZ // 2) % NZ
     line_diag, columns = running_diags(block_diags, NZ, held, start)
@@ -527,10 +525,9 @@
     def line_fill(got_all):
         loop(inner_done, 12, unit)
         later_units(done, done + 8)
-        all_sent(before_line)
 
     got_all = ring(mine_t, lines, line_diags, NY, y, y_next, y_prev, t_send, t_recv, td_send, td_recv, False,
-                   [line_fill, lambda _: later_units(done + 8, done + 12), lambda _: None])
+                   [line_fill, lambda _: later_units(done + 8, done + 12), lambda _: all_sent(before_line)])
     later_units(done + 12, done + 28)
 
     for d in range(1, NY):

time: 74.1 us -> 73.9 us (level)
  no operation moved by 1% of the time
where the time goes in v5:
time: 73.9 us; the launch traced here: 73.8 us
  Pallas kernels  73.8 us (100%)
    pallas_call x1, Pallas kernels, per_device(): pl.pallas_call(body, out_shape=[jax.ShapeDtypeStruct(gradients.shape, F32...  72.2 us
    pallas_call x1, Pallas kernels, per_device(): pl.pallas_call(finish, out_shape=jax.ShapeDtypeStruct(gradients.shape, F3...  1.65 us

profile of v5, /device:TPU:1, one launch (start us, length us, event | category | flops | bytes accessed | tf_op | source)
XLA Modules:
  0.0 73.8 jit_solution(11724565562414140793)
XLA Ops:
  0.0 72.2 %shard_map.28 = (f32[8,128,512]{2,1,0:T(8,128)S(1)}, bf16[512,512]{1,0:T(8,128)(2,1)S(1)}, f32[1,512]{1,0:T(1,128)S(1)}) custom-call(bf16[8,128,512]{2,1,0:T(8,128)(2,1)} %g_hbm.1, f32[8]{0:T(128)} %rate_hbm.1), custom_call_target="tpu_custom_call" | custom-call | tf_op jit(solution)/shard_map/pallas_call | solution.py:570
  72.2 1.7 %shard_map.29 = f32[8,128,512]{2,1,0:T(8,128)} custom-call(f32[8,128,512]{2,1,0:T(8,128)S(1)} %get-tuple-element.8.x_ref, bf16[512,512]{1,0:T(8,128)(2,1)S(1)} %get-tuple-element.9.off_ref, f32[1,512]{1,0:T(1,128)S(1)} %get-tuple-element.10.diag_ref), custom_call_target="tpu_custom_call" | custom-call | tf_op jit(solution)/shard_map/pallas_call | solution.py:604

commit v6 on v5

--- a/solution.py
+++ b/solution.py
@@ -298,12 +298,16 @@
         got_pack(from_left, 2 + which)
         send_pack(from_left, 2 + which, right)
     for which in range(2):
+        unpack_part(from_right, which)
+        unpack_part(from_left, 2 + which)
+    for which in range(2):
         got_pack(from_right, 2 + which)
         got_pack(from_left, which)
     send_pack(from_right, 4, sib)
     send_pack(from_left, 4, sib)
-    unpack(from_right)
-    unpack(from_left)
+    for which in range(2):
+        unpack_part(from_right, 2 + which)
+        unpack_part(from_left, which)
 
     @pl.when(c == 1)
     def _():

time: 73.9 us -> 73.9 us (level)
  no operation moved by 1% of the time
where the time goes in v6:
time: 73.9 us; the launch traced here: 73.8 us
  Pallas kernels  73.8 us (100%)
    pallas_call x1, Pallas kernels, per_device(): pl.pallas_call(body, out_shape=[jax.ShapeDtypeStruct(gradients.shape, F32...  72.2 us
    pallas_call x1, Pallas kernels, per_device(): pl.pallas_call(finish, out_shape=jax.ShapeDtypeStruct(gradients.shape, F3...  1.65 us

profile of v6, /device:TPU:1, one launch (start us, length us, event | category | flops | bytes accessed | tf_op | source)
XLA Modules:
  0.0 73.8 jit_solution(7650603828082815760)
XLA Ops:
  0.0 72.2 %shard_map.28 = (f32[8,128,512]{2,1,0:T(8,128)S(1)}, bf16[512,512]{1,0:T(8,128)(2,1)S(1)}, f32[1,512]{1,0:T(1,128)S(1)}) custom-call(bf16[8,128,512]{2,1,0:T(8,128)(2,1)} %g_hbm.1, f32[8]{0:T(128)} %rate_hbm.1), custom_call_target="tpu_custom_call" | custom-call | tf_op jit(solution)/shard_map/pallas_call | solution.py:574
  72.2 1.7 %shard_map.29 = f32[8,128,512]{2,1,0:T(8,128)} custom-call(f32[8,128,512]{2,1,0:T(8,128)S(1)} %get-tuple-element.8.x_ref, bf16[512,512]{1,0:T(8,128)(2,1)S(1)} %get-tuple-element.9.off_ref, f32[1,512]{1,0:T(1,128)S(1)} %get-tuple-element.10.diag_ref), custom_call_target="tpu_custom_call" | custom-call | tf_op jit(solution)/shard_map/pallas_call | solution.py:608
